TPU v7x, 256 devices: a whole 4x4x8 slice. The times are simulated.
256 devices in a mesh: expert: 64 (over z, x, core), tensor: 4 (over y).
Axes of the slice: x: 4, y: 4, z: 8, core: 2. Of those that a mesh axis runs over, the one named last changes fastest.
Arguments:
- tokens: bfloat16 [16384, 1024], P('expert'), may hold values from -6 to 6
- routes: int32 [16384, 2], P('expert'), may hold values from 0 to 63, all different within a row; in each aligned block of 256 rows (0 to 255, 256 to 511, ...) at most 16 rows name the same one
- mix_weights: float32 [16384, 2], P('expert'), may hold values from 0.2 to 1
- w_gate: bfloat16 [64, 1024, 2048], P('expert', None, 'tensor'), may hold values from -0.1875 to 0.1875
- w_up: bfloat16 [64, 1024, 2048], P('expert', None, 'tensor'), may hold values from -0.1875 to 0.1875
- w_down: bfloat16 [64, 2048, 1024], P('expert', 'tensor'), may hold values from -0.125 to 0.125
- cotangent: bfloat16 [16384, 1024], P('expert'), may hold values from -6 to 6
Outputs:
- result: bfloat16 [16384, 1024], P('expert')
- grad_tokens: bfloat16 [16384, 1024], P('expert')
- grad_gate: float32 [64, 1024, 2048], P('expert', None, 'tensor')
- grad_up: float32 [64, 1024, 2048], P('expert', None, 'tensor')
- grad_down: float32 [64, 2048, 1024], P('expert', 'tensor')
Inputs may be any that keep to these rules, and one draw needn't show every extreme that they name: `routes`: each row names two different experts. Within each aligned block of 256 rows no expert is named by more than 16 rows, a bound that some block reaches.
All inputs are finite; a program needn't handle non-finite values.
Results may differ from a plain program's by a relative error of at most 0.015.
Values may be sent and summed in bfloat16 or wider, within the bound.
No kernel may reach another device: no remote copies, remote signals or barrier semaphores. Data moves between devices by JAX's collectives and lax.ppermute only.
A program may use at most 128 MiB of HBM per device.

v0:
```python
import jax
import jax.numpy as jnp
from jax import lax
from jax.sharding import PartitionSpec as P


def slot_positions(routes, experts, capacity):
    flat_ids = routes.reshape(-1)
    onehot = (flat_ids[:, None] == jnp.arange(experts, dtype=jnp.int32)[None, :]).astype(jnp.int32)
    slot_rank = jnp.sum((jnp.cumsum(onehot, axis=0) - 1) * onehot, axis=1)
    return flat_ids * capacity + slot_rank


def place_rows(values, position, buffer_rows):
    return jnp.zeros((buffer_rows, values.shape[1]), values.dtype).at[position].set(values)


def gather_rows(buffer, position, weights):
    picked = buffer[position].astype(jnp.float32).reshape(weights.shape[0], 2, buffer.shape[1])
    return jnp.sum(picked * weights[:, :, None], axis=1)


def expert_forward(received, gate_local, up_local, down_local):
    pre_gate = jnp.dot(received, gate_local, preferred_element_type=jnp.float32)
    pre_up = jnp.dot(received, up_local, preferred_element_type=jnp.float32)
    hidden = (jax.nn.silu(pre_gate) * pre_up).astype(jnp.bfloat16)
    partial_out = jnp.dot(hidden, down_local, preferred_element_type=jnp.float32)
    return (pre_gate, pre_up, hidden, partial_out)


def expert_backward(received, upstream, pre_gate, pre_up, hidden, gate_local, up_local, down_local):
    contract_last = (((1,), (1,)), ((), ()))
    contract_first = (((0,), (0,)), ((), ()))
    d_hidden = lax.dot_general(
        upstream, down_local, contract_last, preferred_element_type=jnp.float32
    )
    sigma = jax.nn.sigmoid(pre_gate)
    d_gate = (d_hidden * pre_up * sigma * (1.0 + pre_gate * (1.0 - sigma))).astype(jnp.bfloat16)
    d_up = (d_hidden * pre_gate * sigma).astype(jnp.bfloat16)
    grad_down = lax.dot_general(
        hidden, upstream, contract_first, preferred_element_type=jnp.float32
    )
    grad_gate = lax.dot_general(
        received, d_gate, contract_first, preferred_element_type=jnp.float32
    )
    grad_up = lax.dot_general(received, d_up, contract_first, preferred_element_type=jnp.float32)
    partial_in = lax.dot_general(
        d_gate, gate_local, contract_last, preferred_element_type=jnp.float32
    )
    partial_in = partial_in + lax.dot_general(
        d_up, up_local, contract_last, preferred_element_type=jnp.float32
    )
    return (grad_gate, grad_up, grad_down, partial_in)


def shards(tokens, routes, mix_weights, w_gate, w_up, w_down, cotangent):
    experts = lax.axis_size("expert")
    tok_rows = tokens.shape[0]
    feature_width = tokens.shape[1]
    capacity = 4 * tok_rows // experts
    buffer_rows = experts * capacity
    position = slot_positions(routes, experts, capacity)
    gate_local = w_gate[0]
    up_local = w_up[0]
    down_local = w_down[0]
    doubled = jnp.repeat(tokens, 2, axis=0)
    scaled = (mix_weights[:, :, None] * cotangent.astype(jnp.float32)[:, None, :]).astype(
        jnp.bfloat16
    )
    scaled = scaled.reshape(2 * tok_rows, feature_width)
    ones_weights = jnp.ones_like(mix_weights)
    sent = place_rows(doubled, position, buffer_rows).reshape(experts, capacity, feature_width)
    received = lax.all_to_all(sent, "expert", split_axis=0, concat_axis=0, tiled=True).reshape(
        buffer_rows, feature_width
    )
    pre_gate, pre_up, hidden, partial_out = expert_forward(
        received, gate_local, up_local, down_local
    )
    out_full = lax.psum(partial_out.astype(jnp.bfloat16), "tensor")
    back = lax.all_to_all(
        out_full.reshape(experts, capacity, feature_width),
        "expert",
        split_axis=0,
        concat_axis=0,
        tiled=True,
    )
    result = gather_rows(back.reshape(buffer_rows, feature_width), position, mix_weights).astype(
        jnp.bfloat16
    )
    sent_grad = place_rows(scaled, position, buffer_rows).reshape(experts, capacity, feature_width)
    upstream = lax.all_to_all(sent_grad, "expert", split_axis=0, concat_axis=0, tiled=True).reshape(
        buffer_rows, feature_width
    )
    grad_gate, grad_up, grad_down, partial_in = expert_backward(
        received, upstream, pre_gate, pre_up, hidden, gate_local, up_local, down_local
    )
    in_full = lax.psum(partial_in.astype(jnp.bfloat16), "tensor")
    back_in = lax.all_to_all(
        in_full.reshape(experts, capacity, feature_width),
        "expert",
        split_axis=0,
        concat_axis=0,
        tiled=True,
    )
    grad_tokens = gather_rows(
        back_in.reshape(buffer_rows, feature_width), position, ones_weights
    ).astype(jnp.bfloat16)
    return (result, grad_tokens, grad_gate[None], grad_up[None], grad_down[None])


def solution(mesh):
    in_specs = (
        P("expert", None),
        P("expert", None),
        P("expert", None),
        P("expert", None, "tensor"),
        P("expert", None, "tensor"),
        P("expert", "tensor", None),
        P("expert", None),
    )
    out_specs = (
        P("expert", None),
        P("expert", None),
        P("expert", None, "tensor"),
        P("expert", None, "tensor"),
        P("expert", "tensor", None),
    )
    return jax.shard_map(shards, mesh=mesh, in_specs=in_specs, out_specs=out_specs, check_vma=False)
```

profile of v0, /device:TPU:1, one launch (start us, length us, event | category | flops | bytes accessed | tf_op | source)
XLA Modules:
  0.0 376.4 jit_solution(2873069320770572478)
XLA Ops:
  7.2 0.0 copy-start
  7.2 0.9 copy.14
  8.1 0.1 eq.29
  8.2 0.1 eq.25
  8.4 0.7 broadcast_multiply_fusion
  9.1 1.2 reduce-window.6
  10.3 0.2 slice_reduce_fusion
  10.6 0.1 copy.13
  10.7 0.1 mul.72
  10.9 1.6 broadcast_in_dim.8
  12.4 0.4 reshape.127
  12.9 0.1 fusion.16
  13.0 4.1 %scatter_custom_fusion = bf16[1024,1024]{1,0:T(8,128)(2,1)} fusion(s32[512]{0:T(512)S(1)} %bitcast.68, bf16[512,1024]{1,0:T(8,128)(2,1)S(1)} %reshape.127, bf16[]{:T(256)} %constant.7.clone.1), kind=kCustom, calls=%fused_computation.28 | custom fusion | bytes 2097154 | tf_op jit(solution)/shard_map/scatter | solution.py:15
  17.1 0.0 copy-start.7
  17.1 13.3 %all-to-all-start = ((bf16[64,16,1024]{2,1,0:T(8,128)(2,1)}), bf16[64,16,1024]{2,1,0:T(8,128)(2,1)}, u32[]{:S(2)}, u32[]{:S(2)}) async-start(bf16[64,16,1024]{2,1,0:T(8,128)(2,1)} %bitcast.3), calls=%async_computation | async-start | bytes 4194304 | tf_op jit(solution)/shard_map/all_to_all | solution.py:73
  30.5 0.0 copy-done.7
  30.5 0.1 copy.17
  30.6 0.1 mul.78
  30.8 1.6 mul.80
  32.4 2.4 mul.81
  34.8 5.2 %scatter_custom_fusion.1 = bf16[1024,1024]{1,0:T(8,128)(2,1)} fusion(s32[512]{0:T(512)S(1)} %bitcast.69, f32[512,1024]{1,0:T(8,128)} %mul.81, f32[512]{0:T(512)S(1)} %mul.78, bf16[]{:T(256)} %constant.7.clone.1), kind=kCustom, calls=%fused_computation.15 | custom fusion | flops 1048576 | bytes 4196354 | tf_op jit(solution)/shard_map/scatter | solution.py:15
  40.0 40.0 %all-to-all-done = bf16[64,16,1024]{2,1,0:T(8,128)(2,1)} async-done(((bf16[64,16,1024]{2,1,0:T(8,128)(2,1)}), bf16[64,16,1024]{2,1,0:T(8,128)(2,1)}, u32[]{:S(2)}, u32[]{:S(2)}) %all-to-all-start) | async-done | bytes 2097184 | tf_op jit(solution)/shard_map/all_to_all | solution.py:73
  80.1 7.0 %all-to-all-start.2 = ((bf16[64,16,1024]{2,1,0:T(8,128)(2,1)}), bf16[64,16,1024]{2,1,0:T(8,128)(2,1)S(1)}, u32[]{:S(2)}, u32[]{:S(2)}) async-start(bf16[64,16,1024]{2,1,0:T(8,128)(2,1)} %bitcast.64), calls=%async_computation.2 | async-start | bytes 4194304 | tf_op jit(solution)/shard_map/all_to_all | solution.py:91
  87.1 0.2 all-reduce.3.cloned.1.call-start
  87.3 0.0 copy-start.8
  87.3 4.5 %fusion.5 = f32[1024,512]{1,0:T(8,128)} fusion(bf16[1024,1024]{1,0:T(8,128)(2,1)} %bitcast.4, bf16[1,1024,512]{2,1,0:T(8,128)(2,1)} %param.11), kind=kOutput, calls=%fused_computation.20 | convolution fusion | flops 1073741824 | bytes 5242880 | tf_op jit(solution)/shard_map/dot_general | solution.py:25
  91.8 0.0 copy-done.8
  91.9 4.2 %fusion.9 = f32[1024,512]{1,0:T(8,128)} fusion(bf16[1024,1024]{1,0:T(8,128)(2,1)} %bitcast.4, bf16[1,1024,512]{2,1,0:T(8,128)(2,1)S(1)} %copy-done.8), kind=kOutput, calls=%fused_computation.24 | convolution fusion | flops 1073741824 | bytes 5242880 | tf_op jit(solution)/shard_map/dot_general | solution.py:24
  96.0 40.7 %all-to-all-done.2 = bf16[64,16,1024]{2,1,0:T(8,128)(2,1)S(1)} async-done(((bf16[64,16,1024]{2,1,0:T(8,128)(2,1)}), bf16[64,16,1024]{2,1,0:T(8,128)(2,1)S(1)}, u32[]{:S(2)}, u32[]{:S(2)}) %all-to-all-start.2) | async-done | bytes 2097184 | tf_op jit(solution)/shard_map/all_to_all | solution.py:91
  136.8 0.0 copy-start.1
  136.8 0.0 copy-done
  136.8 0.0 copy-start.9
  136.8 5.1 %multiply_convert_fusion = (bf16[1024,512]{1,0:T(8,128)(2,1)S(1)}, bf16[1024,512]{1,0:T(8,128)(2,1)S(1)}, bf16[1024,512]{1,0:T(8,128)(2,1)S(1)}) fusion(f32[1024,512]{1,0:T(8,128)} %fusion.9, f32[1024,512]{1,0:T(8,128)} %fusion.5, bf16[1024,1024]{1,0:T(8,128)(2,1)S(1)} %bitcast.62, bf16[1,512,1024]{2,1,0:T(8,128)(2,1)S(1)} %copy-done), kind=kOutput, calls=%fused_computation.5 | convolution fusion | flops 1082130432 | bytes 10485760 | tf_op jit(solution)/shard_map/dot_general | solution.py:34
  141.9 0.0 copy-done.1
  141.9 0.0 copy-start.10
  141.9 0.0 copy-start.3
  141.9 0.0 copy-start.6
  141.9 0.0 copy-done.9
  141.9 1.3 fusion.7
  143.2 0.0 copy-done.10
  143.2 0.0 copy-done.3
  143.2 0.0 copy-start.5
  143.3 2.6 convolution_convert_fusion
  145.9 0.0 copy-done.6
  145.9 0.0 copy-done.5
  145.9 2.6 add_convert_fusion
  148.5 0.0 all-reduce.3.cloned.1.call-update
  148.5 96.1 %all-reduce.3.cloned.1.call-done = (bf16[64,16,1024]{2,1,0:T(8,128)(2,1)}, bf16[64,16,1024]{2,1,0:T(8,128)(2,1)}) async-done(((bf16[64,16,1024]{2,1,0:T(8,128)(2,1)}, bf16[64,16,1024]{2,1,0:T(8,128)(2,1)}), (bf16[64,16,1024]{2,1,0:T(8,128)(2,1)}, bf16[64,16,1024]{2,1,0:T(8,128)(2,1)})) %all-reduce.3.cloned.1.call-update) | async-done | bytes 4194320 | tf_op jit(solution)/shard_map/psum | solution.py:79
  244.6 60.4 %all_to_all.20 = bf16[64,16,1024]{2,1,0:T(8,128)(2,1)} all-to-all(bf16[64,16,1024]{2,1,0:T(8,128)(2,1)} %get-tuple-element.5), channel_id=1, replica_groups=mesh['expert'=64,'tensor'=4] {'expert'}, dimensions={0} | all-to-all | bytes 4194304 | tf_op jit(solution)/shard_map/all_to_all | solution.py:80
  305.0 7.0 %all-to-all-start.3 = ((bf16[64,16,1024]{2,1,0:T(8,128)(2,1)}), bf16[64,16,1024]{2,1,0:T(8,128)(2,1)S(1)}, u32[]{:S(2)}, u32[]{:S(2)}) async-start(bf16[64,16,1024]{2,1,0:T(8,128)(2,1)} %get-tuple-element.6), calls=%async_computation.3 | async-start | bytes 4194304 | tf_op jit(solution)/shard_map/all_to_all | solution.py:98
  312.1 0.0 copy-start.11
  312.1 4.5 %convolution_bitcast_fusion.1 = f32[1,1024,512]{2,1,0:T(8,128)} fusion(bf16[1024,1024]{1,0:T(8,128)(2,1)} %bitcast.4, bf16[1024,512]{1,0:T(8,128)(2,1)} %copy-done.6), kind=kOutput, calls=%fused_computation.13 | convolution fusion | flops 1073741824 | bytes 5242880 | tf_op jit(solution)/shard_map/dot_general | solution.py:46
  316.6 0.0 copy-done.11
  316.7 4.3 %convolution_bitcast_fusion.2 = f32[1,1024,512]{2,1,0:T(8,128)} fusion(bf16[1024,1024]{1,0:T(8,128)(2,1)} %bitcast.4, bf16[1024,512]{1,0:T(8,128)(2,1)S(1)} %copy-done.11), kind=kOutput, calls=%fused_computation.14 | convolution fusion | flops 1073741824 | bytes 5242880 | tf_op jit(solution)/shard_map/dot_general | solution.py:43
  321.0 0.0 copy-done.2
  321.0 0.0 copy-done.4
  321.0 2.6 convolution_bitcast_fusion
  323.6 5.4 %gather_fusion = bf16[512,1024]{1,0:T(8,128)(2,1)} fusion(bf16[1024,1024]{1,0:T(8,128)(2,1)} %bitcast.61, s32[1024]{0:T(1024)S(1)} %pad_clamp_fusion), kind=kCustom, calls=%fused_computation | custom fusion | bytes 2099200 | tf_op jit(solution)/shard_map/gather | solution.py:19
  328.9 3.3 reshape.106
  332.3 5.1 %multiply_reduce_fusion = bf16[256,1024]{1,0:T(8,128)(2,1)} fusion(f32[256,2,1024]{2,1,0:T(2,128)} %reshape.106, f32[256,2]{1,0:T(8,128)S(1)} %copy.17), kind=kLoop, calls=%fused_computation.8 | loop fusion | flops 786432 | bytes 2623488 | tf_op jit(solution)/shard_map/reduce_sum | solution.py:20
  337.4 24.3 %all-to-all-done.3 = bf16[64,16,1024]{2,1,0:T(8,128)(2,1)S(1)} async-done(((bf16[64,16,1024]{2,1,0:T(8,128)(2,1)}), bf16[64,16,1024]{2,1,0:T(8,128)(2,1)S(1)}, u32[]{:S(2)}, u32[]{:S(2)}) %all-to-all-start.3) | async-done | bytes 2097184 | tf_op jit(solution)/shard_map/all_to_all | solution.py:98
  361.7 2.8 gather_fusion.1
  364.5 1.5 gather.10
  366.0 3.6 reduce_sum.35
  (7 shorter events, 0.1 us)
Async XLA Ops:
  7.2 129.6 %copy-start = (bf16[1,512,1024]{2,1,0:T(8,128)(2,1)S(1)}, bf16[1,512,1024]{2,1,0:T(8,128)(2,1)}, u32[]{:S(2)}) copy-start(bf16[1,512,1024]{2,1,0:T(8,128)(2,1)} %param.12) | copy-start | bytes 3145732
  17.1 13.3 %copy-start.7 = (f32[256,2]{0,1:T(2,128)S(1)}, f32[256,2]{0,1:T(2,128)}, u32[]{:S(2)}) copy-start(f32[256,2]{0,1:T(2,128)} %param.9) | copy-start | bytes 6148
  17.1 62.9 %all-to-all-start = ((bf16[64,16,1024]{2,1,0:T(8,128)(2,1)}), bf16[64,16,1024]{2,1,0:T(8,128)(2,1)}, u32[]{:S(2)}, u32[]{:S(2)}) async-start(bf16[64,16,1024]{2,1,0:T(8,128)(2,1)} %bitcast.3), calls=%async_computation | async-start | bytes 4194304 | tf_op jit(solution)/shard_map/all_to_all | solution.py:73
  80.1 56.7 %all-to-all-start.2 = ((bf16[64,16,1024]{2,1,0:T(8,128)(2,1)}), bf16[64,16,1024]{2,1,0:T(8,128)(2,1)S(1)}, u32[]{:S(2)}, u32[]{:S(2)}) async-start(bf16[64,16,1024]{2,1,0:T(8,128)(2,1)} %bitcast.64), calls=%async_computation.2 | async-start | bytes 4194304 | tf_op jit(solution)/shard_map/all_to_all | solution.py:91
  87.1 157.5 %all-reduce.3.cloned.1.call-start = ((), (), s32[]{:S(2)}) async-start(), calls=%async_computation.4 | async-start | bytes 8388608 | tf_op jit(solution)/shard_map/psum | solution.py:79
  87.3 4.5 %copy-start.8 = (bf16[1,1024,512]{2,1,0:T(8,128)(2,1)S(1)}, bf16[1,1024,512]{2,1,0:T(8,128)(2,1)}, u32[]{:S(2)}) copy-start(bf16[1,1024,512]{2,1,0:T(8,128)(2,1)} %param.10) | copy-start | bytes 3145732
  136.8 5.1 %copy-start.1 = (bf16[64,16,1024]{2,1,0:T(8,128)(2,1)}, bf16[64,16,1024]{2,1,0:T(8,128)(2,1)S(1)}, u32[]{:S(2)}) copy-start(bf16[64,16,1024]{2,1,0:T(8,128)(2,1)S(1)} %all-to-all-done.2) | copy-start | bytes 6291460
  136.8 5.2 %copy-start.9 = (bf16[1,1024,512]{2,1,0:T(8,128)(2,1)S(1)}, bf16[1,1024,512]{2,1,0:T(8,128)(2,1)}, u32[]{:S(2)}) copy-start(bf16[1,1024,512]{2,1,0:T(8,128)(2,1)} %param.10) | copy-start | bytes 3145732
  141.9 1.3 copy-start.10
  141.9 1.3 copy-start.3
  141.9 3.9 %copy-start.6 = (bf16[1024,512]{1,0:T(8,128)(2,1)}, bf16[1024,512]{1,0:T(8,128)(2,1)S(1)}, u32[]{:S(2)}) copy-start(bf16[1024,512]{1,0:T(8,128)(2,1)S(1)} %get-tuple-element.7) | copy-start | bytes 3145732
  143.2 2.6 copy-start.5
  305.0 56.7 %all-to-all-start.3 = ((bf16[64,16,1024]{2,1,0:T(8,128)(2,1)}), bf16[64,16,1024]{2,1,0:T(8,128)(2,1)S(1)}, u32[]{:S(2)}, u32[]{:S(2)}) async-start(bf16[64,16,1024]{2,1,0:T(8,128)(2,1)} %get-tuple-element.6), calls=%async_computation.3 | async-start | bytes 4194304 | tf_op jit(solution)/shard_map/all_to_all | solution.py:98
  312.1 4.6 %copy-start.11 = (bf16[1024,512]{1,0:T(8,128)(2,1)S(1)}, bf16[1024,512]{1,0:T(8,128)(2,1)}, u32[]{:S(2)}) copy-start(bf16[1024,512]{1,0:T(8,128)(2,1)} %copy-done.10) | copy-start | bytes 3145732
  316.7 4.3 %copy-start.2 = (bf16[64,16,1024]{2,1,0:T(8,128)(2,1)S(1)}, bf16[64,16,1024]{2,1,0:T(8,128)(2,1)}, u32[]{:S(2)}) copy-start(bf16[64,16,1024]{2,1,0:T(8,128)(2,1)} %copy-done.1) | copy-start | bytes 6291460
  316.7 4.3 %copy-start.4 = (bf16[1024,512]{1,0:T(8,128)(2,1)S(1)}, bf16[1024,512]{1,0:T(8,128)(2,1)}, u32[]{:S(2)}) copy-start(bf16[1024,512]{1,0:T(8,128)(2,1)} %copy-done.3) | copy-start | bytes 3145732
Sparse Core Ops, SparseCore 0:
  148.6 95.9 all-reduce.2
where the time goes:
time: 378 us; the launch traced here: 376 us
  waiting for transfers between devices  201 us (53%)
  blocking collectives  60.4 us (16%)
  matrix products  31.8 us (8%)
  starting transfers between devices  27.6 us (7%)
  local copies, waits for them, and re-layouts  25.2 us (7%)
  other arithmetic  16 us (4%)
  between operations  14.3 us (4%)
    psum x1, waiting for transfers between devices, shards(): out_full = lax.psum(partial_out.astype(jnp.bfloat16), 'tensor')  96.1 us
    all_to_all x1, blocking collectives, shards(): lax.all_to_all(out_full.reshape(experts, capacity, feature_width), 'exper...  60.4 us
    all_to_all x1, waiting for transfers between devices, shards(): lax.all_to_all(sent_grad, 'expert', split_axis=0, concat_axis=0, tiled=True)  40.7 us
    all_to_all x1, waiting for transfers between devices, shards(): lax.all_to_all(sent, 'expert', split_axis=0, concat_axis=0, tiled=True)  40 us
    all_to_all x1, waiting for transfers between devices, shards(): lax.all_to_all(in_full.reshape(experts, capacity, feature_width), 'expert...  24.3 us
    all_to_all x1, starting transfers between devices, shards(): lax.all_to_all(sent, 'expert', split_axis=0, concat_axis=0, tiled=True)  13.3 us
    gather x3, local copies, waits for them, and re-layouts, gather_rows(): buffer[position].astype(jnp.float32)  9.6 us
    reduce_sum x2, other arithmetic, gather_rows(): return jnp.sum(picked * weights[:, :, None], axis=1)  8.72 us
  transfers between devices with their start and end apart: 4, of which 4 were waited for; matrix products, arithmetic and copies ran while one was open for 12% of the time, Pallas kernels for 0%

commit v1 on v0

v1 whole, which is shorter than its diff:
```python
import functools

import jax
import jax.numpy as jnp
from jax import lax
from jax.experimental import pallas as pl
from jax.experimental.pallas import tpu as pltpu
from jax.sharding import PartitionSpec as P

F32 = jnp.float32
BF16 = jnp.bfloat16
NN = (((1,), (0,)), ((), ()))
NT = (((1,), (1,)), ((), ()))
TN = (((0,), (0,)), ((), ()))


def dot(a, b, dims):
    return lax.dot_general(a, b, dims, preferred_element_type=F32)


def places(routes, experts, capacity):
    rows = routes.shape[0]
    first, second = routes[:, 0:1], routes[:, 1:2]
    lanes = lax.broadcasted_iota(jnp.int32, (rows, experts), 1)
    hot0 = (lanes == first).astype(F32)
    hot1 = (lanes == second).astype(F32)
    before = (
        lax.broadcasted_iota(jnp.int32, (rows, rows), 1)
        < lax.broadcasted_iota(jnp.int32, (rows, rows), 0)
    ).astype(F32)
    earlier = dot(before.astype(BF16), (hot0 + hot1).astype(BF16), NN)
    rank0 = jnp.sum(earlier * hot0, axis=1, keepdims=True)
    rank1 = jnp.sum((earlier + hot0) * hot1, axis=1, keepdims=True)
    return (
        first * capacity + rank0.astype(jnp.int32),
        second * capacity + rank1.astype(jnp.int32),
    )


def one_hot(place, width):
    lanes = lax.broadcasted_iota(jnp.int32, (place.shape[0], width), 1)
    return (lanes == place).astype(F32).astype(BF16)


def dispatch_kernel(capacity, experts, me, routes, mix, tokens, cotangent, x_out, g_out):
    place0, place1 = places(routes[...], experts, capacity)
    buffer_rows = experts * capacity
    pick0, pick1 = one_hot(place0, buffer_rows), one_hot(place1, buffer_rows)
    x_out[...] = dot(pick0 + pick1, tokens[...], TN).astype(BF16)
    cot = cotangent[...].astype(F32)
    weights = mix[...]
    scaled0 = (weights[:, 0:1] * cot).astype(BF16)
    scaled1 = (weights[:, 1:2] * cot).astype(BF16)
    g_out[...] = (dot(pick0, scaled0, TN) + dot(pick1, scaled1, TN)).astype(BF16)


def dispatch(member, routes, mix, tokens, cotangent, experts, capacity, parts):
    rows, width = tokens.shape[0], tokens.shape[1] // parts
    whole = lambda i, me: (0, 0)
    mine = lambda i, me: (0, me[0])
    out = jax.ShapeDtypeStruct((experts * capacity, width), BF16)
    return pl.pallas_call(
        functools.partial(dispatch_kernel, capacity, experts),
        grid_spec=pltpu.PrefetchScalarGridSpec(
            num_scalar_prefetch=1,
            grid=(1,),
            in_specs=[
                pl.BlockSpec((rows, 2), whole),
                pl.BlockSpec((rows, 2), whole),
                pl.BlockSpec((rows, width), mine),
                pl.BlockSpec((rows, width), mine),
            ],
            out_specs=[pl.BlockSpec((experts * capacity, width), whole)] * 2,
        ),
        out_shape=(out, out),
        compiler_params=pltpu.CompilerParams(vmem_limit_bytes=32 << 20),
        name="dispatch",
    )(member, routes, mix, tokens, cotangent)


def forward_kernel(parts, x, w_gate, w_up, w_down, pre_gate, pre_up, hidden, partial_out):
    width = x.shape[2]
    gate = up = None
    for t in range(parts):
        rows = pl.ds(t * width, width)
        g = dot(x[t], w_gate[0, rows, :], NN)
        u = dot(x[t], w_up[0, rows, :], NN)
        gate, up = (g, u) if gate is None else (gate + g, up + u)
    pre_gate[...] = gate
    pre_up[...] = up
    act = (gate / (1.0 + jnp.exp(-gate)) * up).astype(BF16)
    hidden[...] = act
    for t in range(parts):
        partial_out[t] = dot(act, w_down[0, :, pl.ds(t * width, width)], NN).astype(BF16)


def forward(x, w_gate, w_up, w_down, block):
    parts, rows, width = x.shape
    units = w_gate.shape[2]
    fixed = lambda i: (0, 0, 0)
    chunk = pl.BlockSpec((parts, block, width), lambda i: (0, i, 0))
    tall = pl.BlockSpec((block, units), lambda i: (i, 0))
    return pl.pallas_call(
        functools.partial(forward_kernel, parts),
        grid=(rows // block,),
        in_specs=[
            chunk,
            pl.BlockSpec(w_gate.shape, fixed),
            pl.BlockSpec(w_up.shape, fixed),
            pl.BlockSpec(w_down.shape, fixed),
        ],
        out_specs=[tall, tall, tall, chunk],
        out_shape=(
            jax.ShapeDtypeStruct((rows, units), F32),
            jax.ShapeDtypeStruct((rows, units), F32),
            jax.ShapeDtypeStruct((rows, units), BF16),
            jax.ShapeDtypeStruct((parts, rows, width), BF16),
        ),
        compiler_params=pltpu.CompilerParams(vmem_limit_bytes=48 << 20),
        cost_estimate=pl.CostEstimate(
            flops=6 * rows * parts * width * units, bytes_accessed=12 << 20, transcendentals=rows * units
        ),
        name="forward",
    )(x, w_gate, w_up, w_down)


def backward_kernel(parts, g, pre_gate, pre_up, w_gate, w_up, w_down, d_gate, d_up, partial_in):
    width = g.shape[2]
    d_hidden = None
    for t in range(parts):
        part = dot(g[t], w_down[0, :, pl.ds(t * width, width)], NT)
        d_hidden = part if d_hidden is None else d_hidden + part
    gate, up = pre_gate[...], pre_up[...]
    sigma = 1.0 / (1.0 + jnp.exp(-gate))
    dg = (d_hidden * up * sigma * (1.0 + gate * (1.0 - sigma))).astype(BF16)
    du = (d_hidden * gate * sigma).astype(BF16)
    d_gate[...] = dg
    d_up[...] = du
    for t in range(parts):
        rows = pl.ds(t * width, width)
        partial_in[t] = (dot(dg, w_gate[0, rows, :], NT) + dot(du, w_up[0, rows, :], NT)).astype(BF16)


def backward(g, pre_gate, pre_up, w_gate, w_up, w_down, block):
    parts, rows, width = g.shape
    units = w_gate.shape[2]
    fixed = lambda i: (0, 0, 0)
    chunk = pl.BlockSpec((parts, block, width), lambda i: (0, i, 0))
    tall = pl.BlockSpec((block, units), lambda i: (i, 0))
    return pl.pallas_call(
        functools.partial(backward_kernel, parts),
        grid=(rows // block,),
        in_specs=[
            chunk,
            tall,
            tall,
            pl.BlockSpec(w_gate.shape, fixed),
            pl.BlockSpec(w_up.shape, fixed),
            pl.BlockSpec(w_down.shape, fixed),
        ],
        out_specs=[tall, tall, chunk],
        out_shape=(
            jax.ShapeDtypeStruct((rows, units), BF16),
            jax.ShapeDtypeStruct((rows, units), BF16),
            jax.ShapeDtypeStruct((parts, rows, width), BF16),
        ),
        compiler_params=pltpu.CompilerParams(vmem_limit_bytes=48 << 20),
        cost_estimate=pl.CostEstimate(
            flops=6 * rows * parts * width * units, bytes_accessed=13 << 20, transcendentals=rows * units
        ),
        name="backward",
    )(g, pre_gate, pre_up, w_gate, w_up, w_down)


def weights_kernel(x, g, hidden, d_gate, d_up, grad_gate, grad_up, grad_down):
    grad_gate[0] = dot(x[0], d_gate[...], TN)
    grad_up[0] = dot(x[0], d_up[...], TN)
    grad_down[0] = dot(hidden[...], g[0], TN)


def weight_grads(x, g, hidden, d_gate, d_up):
    parts, rows, width = x.shape
    units = hidden.shape[1]
    fixed = pl.BlockSpec((rows, units), lambda t: (0, 0))
    chunk = pl.BlockSpec((1, rows, width), lambda t: (t, 0, 0))
    tall = pl.BlockSpec((1, width, units), lambda t: (0, t, 0))
    return pl.pallas_call(
        weights_kernel,
        grid=(parts,),
        in_specs=[chunk, chunk, fixed, fixed, fixed],
        out_specs=[tall, tall, pl.BlockSpec((1, units, width), lambda t: (0, 0, t))],
        out_shape=(
            jax.ShapeDtypeStruct((1, parts * width, units), F32),
            jax.ShapeDtypeStruct((1, parts * width, units), F32),
            jax.ShapeDtypeStruct((1, units, parts * width), F32),
        ),
        compiler_params=pltpu.CompilerParams(vmem_limit_bytes=48 << 20),
        cost_estimate=pl.CostEstimate(
            flops=6 * rows * parts * width * units, bytes_accessed=13 << 20, transcendentals=0
        ),
        name="weight_grads",
    )(x, g, hidden, d_gate, d_up)


def combine_kernel(capacity, experts, weighted, routes, mix, back, out):
    place0, place1 = places(routes[...], experts, capacity)
    values = back[...]
    first = dot(one_hot(place0, values.shape[0]), values, NN)
    second = dot(one_hot(place1, values.shape[0]), values, NN)
    if weighted:
        first = first * mix[:, 0:1]
        second = second * mix[:, 1:2]
    out[...] = (first + second).astype(BF16)


def combine(routes, mix, back, experts, capacity, weighted):
    return pl.pallas_call(
        functools.partial(combine_kernel, capacity, experts, weighted),
        out_shape=jax.ShapeDtypeStruct((routes.shape[0], back.shape[1]), BF16),
        compiler_params=pltpu.CompilerParams(vmem_limit_bytes=32 << 20),
        name="combine",
    )(routes, mix, back)


def exchange(values, experts, capacity):
    width = values.shape[1]
    moved = lax.all_to_all(
        values.reshape(experts, capacity, width), "expert", split_axis=0, concat_axis=0, tiled=True
    )
    return moved.reshape(experts * capacity, width)


def shards(tokens, routes, mix_weights, w_gate, w_up, w_down, cotangent):
    experts = lax.axis_size("expert")
    parts = lax.axis_size("tensor")
    capacity = 4 * tokens.shape[0] // experts
    block = 256
    member = lax.axis_index("tensor").astype(jnp.int32).reshape(1)
    x_sent, g_sent = dispatch(
        member, routes, mix_weights, tokens, cotangent, experts, capacity, parts
    )
    x_mine = exchange(x_sent, experts, capacity)
    x = lax.all_gather(x_mine, "tensor")
    g_mine = exchange(g_sent, experts, capacity)
    g = lax.all_gather(g_mine, "tensor")
    pre_gate, pre_up, hidden, partial_out = forward(x, w_gate, w_up, w_down, block)
    out_mine = lax.psum_scatter(partial_out, "tensor", scatter_dimension=0, tiled=False)
    d_gate, d_up, partial_in = backward(g, pre_gate, pre_up, w_gate, w_up, w_down, block)
    in_mine = lax.psum_scatter(partial_in, "tensor", scatter_dimension=0, tiled=False)
    grad_gate, grad_up, grad_down = weight_grads(x, g, hidden, d_gate, d_up)
    out_back = exchange(out_mine, experts, capacity)
    result = combine(routes, mix_weights, out_back, experts, capacity, True)
    result = lax.all_gather(result, "tensor", axis=1, tiled=True)
    in_back = exchange(in_mine, experts, capacity)
    grad_tokens = combine(routes, mix_weights, in_back, experts, capacity, False)
    grad_tokens = lax.all_gather(grad_tokens, "tensor", axis=1, tiled=True)
    return (result, grad_tokens, grad_gate, grad_up, grad_down)


def solution(mesh):
    in_specs = (
        P("expert", None),
        P("expert", None),
        P("expert", None),
        P("expert", None, "tensor"),
        P("expert", None, "tensor"),
        P("expert", "tensor", None),
        P("expert", None),
    )
    out_specs = (
        P("expert", None),
        P("expert", None),
        P("expert", None, "tensor"),
        P("expert", None, "tensor"),
        P("expert", "tensor", None),
    )
    return jax.shard_map(shards, mesh=mesh, in_specs=in_specs, out_specs=out_specs, check_vma=False)
```

time: 378 us -> 235 us (0.62)
  waiting for transfers between devices: 201 us -> 82.1 us
  matrix products: 31.8 us -> 0 us
  Pallas kernels: 0 us -> 23.5 us
  other arithmetic: 16 us -> 0 us
  blocking collectives: 60.4 us -> 75.2 us
  local copies, waits for them, and re-layouts: 25.2 us -> 14.3 us
  starting transfers between devices: 27.6 us -> 21.4 us
    all_to_all x3 -> x2, waiting for transfers between devices: 105 us -> 0.01 us  [exchange(): lax.all_to_all(values.reshape(experts, capacity, width), 'expert', split_...]
    psum x1 -> x0, waiting for transfers between devices: 96.1 us -> none  [shards(): out_full = lax.psum(partial_out.astype(jnp.bfloat16), 'tensor')]
    reduce_scatter x0 -> x2, waiting for transfers between devices: none -> 48.8 us  [the longest x1 24.8 us: shards(): lax.psum_scatter(partial_out, 'tensor', scatter_dimension=0, tiled=False)]
    all_gather x0 -> x2, waiting for transfers between devices: none -> 33.2 us  [the longest x1 26.6 us: shards(): g = lax.all_gather(g_mine, 'tensor')]
    dot_general x9 -> x0, matrix products: 31.8 us -> none  [the longest x1 5.12 us: expert_backward(): lax.dot_general(upstream, down_local, contract_last, preferred_element_ty...]
    pallas_call x0 -> x6, Pallas kernels: none -> 23.5 us  [the longest x1 7.5 us: backward(): pl.pallas_call(functools.partial(backward_kernel, parts), grid=(rows // b...]
    all_gather x0 -> x2, blocking collectives: none -> 21.3 us  [the longest x1 11.1 us: shards(): grad_tokens = lax.all_gather(grad_tokens, 'tensor', axis=1, tiled=True)]
    unnamed x26 -> x30, local copies, waits for them, and re-layouts: 1.09 us -> 14.3 us
  transfers between devices with their start and end apart: 4 -> 6, of which waited for: 4 -> 4; matrix products, arithmetic and copies ran while one was open for 12% -> 0% of each run, Pallas kernels for 0% -> 9%
where the time goes in v1:
time: 235 us; the launch traced here: 230 us
  waiting for transfers between devices  82.1 us (35%)
  blocking collectives  75.2 us (32%)
  Pallas kernels  23.5 us (10%)
  starting transfers between devices  21.4 us (9%)
  local copies, waits for them, and re-layouts  14.3 us (6%)
  between operations  13.9 us (6%)
    all_to_all x2, blocking collectives, exchange(): lax.all_to_all(values.reshape(experts, capacity, width), 'expert', split_...  54 us
    all_gather x1, waiting for transfers between devices, shards(): g = lax.all_gather(g_mine, 'tensor')  26.6 us
    reduce_scatter x1, waiting for transfers between devices, shards(): lax.psum_scatter(partial_out, 'tensor', scatter_dimension=0, tiled=False)  24.8 us
    reduce_scatter x1, waiting for transfers between devices, shards(): lax.psum_scatter(partial_in, 'tensor', scatter_dimension=0, tiled=False)  24 us
    all_to_all x2, starting transfers between devices, exchange(): lax.all_to_all(values.reshape(experts, capacity, width), 'expert', split_...  21.2 us
    unnamed x30, local copies, waits for them, and re-layouts  14.3 us
    all_gather x1, blocking collectives, shards(): grad_tokens = lax.all_gather(grad_tokens, 'tensor', axis=1, tiled=True)  11.1 us
    all_gather x1, blocking collectives, shards(): result = lax.all_gather(result, 'tensor', axis=1, tiled=True)  10.2 us
  transfers between devices with their start and end apart: 6, of which 4 were waited for; matrix products, arithmetic and copies ran while one was open for 0% of the time, Pallas kernels for 9%

profile of v1, /device:TPU:1, one launch (start us, length us, event | category | flops | bytes accessed | tf_op | source)
XLA Modules:
  0.0 230.3 jit_solution(860805644614050445)
XLA Ops:
  7.2 0.0 all-gather.3.cloned.1.call-start
  7.2 0.8 copy.20.routes
  8.0 0.8 copy.21.mix
  8.9 0.0 copy-start
  8.9 1.0 copy-done
  9.9 0.0 copy-start.1
  9.9 1.0 copy-done.1
  10.9 0.0 copy-start.3
  10.9 0.0 copy-start.4
  10.9 1.2 dispatch.1
  12.1 30.6 %all_to_all.20 = bf16[64,16,256]{2,1,0:T(8,128)(2,1)} all-to-all(bf16[64,16,256]{2,1,0:T(8,128)(2,1)S(1)} %bitcast.12), channel_id=1, replica_groups=mesh['expert'=64,'tensor'=4] {'expert'}, dimensions={0} | all-to-all | bytes 1048576 | tf_op jit(solution)/shard_map/all_to_all | solution.py:227
  42.8 0.0 all-gather.3.cloned.1.call-update
  42.8 0.0 all-gather.5.cloned.1.call-start
  42.8 23.3 %all_to_all.21 = bf16[64,16,256]{2,1,0:T(8,128)(2,1)} all-to-all(bf16[64,16,256]{2,1,0:T(8,128)(2,1)S(1)} %bitcast.11), channel_id=1, replica_groups=mesh['expert'=64,'tensor'=4] {'expert'}, dimensions={0} | all-to-all | bytes 1048576 | tf_op jit(solution)/shard_map/all_to_all | solution.py:227
  66.2 0.0 all-gather.5.cloned.1.call-update
  66.2 0.0 reduce-scatter.3.cloned.1.call-start
  66.2 6.6 %all-gather.3.cloned.1.call-done.x = bf16[4,1024,256]{2,1,0:T(8,128)(2,1)} async-done(((bf16[1,1024,256]{2,1,0:T(8,128)(2,1)}), bf16[4,1024,256]{2,1,0:T(8,128)(2,1)}) %all-gather.3.cloned.1.call-update) | async-done | bytes 2097168 | tf_op jit(solution)/shard_map/all_gather | solution.py:243
  72.9 0.0 copy-done.3
  72.9 0.0 copy-done.4
  72.9 0.0 copy-start.5
  72.9 1.2 copy-done.5
  74.1 6.4 %forward.1 = (f32[1024,512]{1,0:T(8,128)}, f32[1024,512]{1,0:T(8,128)}, bf16[1024,512]{1,0:T(8,128)(2,1)S(1)}, bf16[4,1024,256]{2,1,0:T(8,128)(2,1)}) custom-call(bf16[4,1024,256]{2,1,0:T(8,128)(2,1)} %all-gather.3.cloned.1.call-done.x, bf16[1,1024,512]{2,1,0:T(8,128)(2,1)S(1)} %copy-done.3, bf16[1,1024,512]{2,1,0:T(8,128)(2,1)S(1)} %copy-done.4, ...), custom_call_target="tpu_custom_call" | custom-call | flops 3221225472 | bytes 12582912 | tf_op jit(solution)/shard_map/forward/pallas_call | solution.py:103
  80.6 0.0 copy-start.11
  80.6 1.0 copy-done.11
  81.5 0.0 reduce-scatter.3.cloned.1.call-update
  81.6 0.0 reduce-scatter.5.cloned.1.call-start
  81.6 26.6 %all-gather.5.cloned.1.call-done.g = bf16[4,1024,256]{2,1,0:T(8,128)(2,1)} async-done(((bf16[1,1024,256]{2,1,0:T(8,128)(2,1)}), bf16[4,1024,256]{2,1,0:T(8,128)(2,1)}) %all-gather.5.cloned.1.call-update) | async-done | bytes 2097168 | tf_op jit(solution)/shard_map/all_gather | solution.py:245
  108.2 0.0 copy-start.6
  108.2 1.2 copy-done.6
  109.4 7.5 %backward.1 = (bf16[1024,512]{1,0:T(8,128)(2,1)S(1)}, bf16[1024,512]{1,0:T(8,128)(2,1)S(1)}, bf16[4,1024,256]{2,1,0:T(8,128)(2,1)}) custom-call(bf16[4,1024,256]{2,1,0:T(8,128)(2,1)} %all-gather.5.cloned.1.call-done.g, f32[1024,512]{1,0:T(8,128)} %get-tuple-element.20.pre_gate, f32[1024,512]{1,0:T(8,128)} %get-tuple-element.21.pre_up, ...), custom_call_target="tpu_custom_call" | custom-call | flops 3221225472 | bytes 13631488 | tf_op jit(solution)/shard_map/backward/pallas_call | solution.py:150
  116.9 0.0 copy-start.7
  116.9 1.0 copy-done.7
  117.9 0.0 copy-start.9
  117.9 1.0 copy-done.9
  118.8 0.0 copy-start.2
  118.9 0.0 reduce-scatter.5.cloned.1.call-update
  118.9 24.8 %reduce-scatter.3.cloned.1.call-done = bf16[1,1024,256]{2,1,0:T(8,128)(2,1)} async-done(((bf16[4,1024,256]{2,1,0:T(8,128)(2,1)}), bf16[1,1024,256]{2,1,0:T(8,128)(2,1)}) %reduce-scatter.3.cloned.1.call-update) | async-done | bytes 524304 | tf_op jit(solution)/shard_map/reduce_scatter | solution.py:247
  143.7 10.6 %all-to-all-start.1 = ((bf16[64,16,256]{2,1,0:T(8,128)(2,1)}), bf16[64,16,256]{2,1,0:T(8,128)(2,1)S(1)}, u32[]{:S(2)}, u32[]{:S(2)}) async-start(bf16[64,16,256]{2,1,0:T(8,128)(2,1)} %bitcast.16), calls=%async_computation.2 | async-start | bytes 1048576 | tf_op jit(solution)/shard_map/all_to_all | solution.py:227
  154.3 24.0 %reduce-scatter.5.cloned.1.call-done = bf16[1,1024,256]{2,1,0:T(8,128)(2,1)} async-done(((bf16[4,1024,256]{2,1,0:T(8,128)(2,1)}), bf16[1,1024,256]{2,1,0:T(8,128)(2,1)}) %reduce-scatter.5.cloned.1.call-update) | async-done | bytes 524304 | tf_op jit(solution)/shard_map/reduce_scatter | solution.py:249
  178.3 0.0 all-to-all-done.1
  178.3 10.6 %all-to-all-start.3 = ((bf16[64,16,256]{2,1,0:T(8,128)(2,1)}), bf16[64,16,256]{2,1,0:T(8,128)(2,1)S(1)}, u32[]{:S(2)}, u32[]{:S(2)}) async-start(bf16[64,16,256]{2,1,0:T(8,128)(2,1)} %bitcast.15), calls=%async_computation.5 | async-start | bytes 1048576 | tf_op jit(solution)/shard_map/all_to_all | solution.py:227
  188.9 0.0 copy-done.2
  188.9 0.0 copy-start.8
  188.9 1.2 copy-done.8
  190.1 0.0 copy-start.10
  190.1 1.2 copy-done.10
  191.3 0.0 copy-start.12
  191.3 1.2 copy-done.12
  192.6 6.3 %weight_grads.1 = (f32[1,1024,512]{2,1,0:T(8,128)}, f32[1,1024,512]{2,1,0:T(8,128)}, f32[1,512,1024]{2,1,0:T(8,128)}) custom-call(bf16[4,1024,256]{2,1,0:T(8,128)(2,1)S(1)} %copy-done.2, bf16[4,1024,256]{2,1,0:T(8,128)(2,1)} %all-gather.5.cloned.1.call-done.g, bf16[1024,512]{1,0:T(8,128)(2,1)S(1)} %copy-done.12, bf16[1024,512]{1,0:T(8,128)(2,1)S(1)} %copy-done.8, ...), custom_call_target="tpu_custom_call" | custom-call | flops 3221225472 | bytes 13631488 | tf_op jit(solution)/shard_map/weight_grads/pallas_call | solution.py:187
  198.9 1.0 combine.2
  199.9 10.2 %all_gather.13 = bf16[256,1024]{1,0:T(8,128)(2,1)S(1)} all-gather(bf16[256,256]{1,0:T(8,128)(2,1)S(1)} %combine.2), channel_id=1, replica_groups=mesh['expert'=64,'tensor'=4] {'tensor'}, dimensions={1}, use_global_device_ids=true | all-gather | bytes 655360 | tf_op jit(solution)/shard_map/all_gather | solution.py:253
  210.1 0.0 all-to-all-done.3
  210.1 1.0 combine.3
  211.1 11.1 %all_gather.15 = bf16[256,1024]{1,0:T(8,128)(2,1)S(1)} all-gather(bf16[256,256]{1,0:T(8,128)(2,1)S(1)} %combine.3), channel_id=1, replica_groups=mesh['expert'=64,'tensor'=4] {'tensor'}, dimensions={1}, use_global_device_ids=true | all-gather | bytes 655360 | tf_op jit(solution)/shard_map/all_gather | solution.py:256
  222.2 0.8 copy.26
  223.0 0.8 copy.27
Async XLA Ops:
  7.2 65.7 %all-gather.3.cloned.1.call-start = ((), (), s32[]{:S(2)}) async-start(), calls=%async_computation.6 | async-start | bytes 2621440 | tf_op jit(solution)/shard_map/all_gather | solution.py:243
  8.9 1.0 copy-start
  9.9 1.0 copy-start.1
  10.9 62.0 %copy-start.3 = (bf16[1,1024,512]{2,1,0:T(8,128)(2,1)S(1)}, bf16[1,1024,512]{2,1,0:T(8,128)(2,1)}, u32[]{:S(2)}) copy-start(bf16[1,1024,512]{2,1,0:T(8,128)(2,1)} %w_gate.3) | copy-start | bytes 3145732
  10.9 62.0 %copy-start.4 = (bf16[1,1024,512]{2,1,0:T(8,128)(2,1)S(1)}, bf16[1,1024,512]{2,1,0:T(8,128)(2,1)}, u32[]{:S(2)}) copy-start(bf16[1,1024,512]{2,1,0:T(8,128)(2,1)} %w_up.3) | copy-start | bytes 3145732
  42.8 65.4 %all-gather.5.cloned.1.call-start = ((), (), s32[]{:S(2)}) async-start(), calls=%async_computation.8 | async-start | bytes 2621440 | tf_op jit(solution)/shard_map/all_gather | solution.py:245
  66.2 77.5 %reduce-scatter.3.cloned.1.call-start = ((), (), s32[]{:S(2)}) async-start(), calls=%async_computation.7 | async-start | bytes 2621440 | tf_op jit(solution)/shard_map/reduce_scatter | solution.py:247
  72.9 1.2 copy-start.5
  80.6 1.0 copy-start.11
  81.6 96.7 %reduce-scatter.5.cloned.1.call-start = ((), (), s32[]{:S(2)}) async-start(), calls=%async_computation.9 | async-start | bytes 2621440 | tf_op jit(solution)/shard_map/reduce_scatter | solution.py:249
  108.2 1.2 copy-start.6
  116.9 1.0 copy-start.7
  117.9 1.0 copy-start.9
  118.8 70.0 %copy-start.2 = (bf16[4,1024,256]{2,1,0:T(8,128)(2,1)S(1)}, bf16[4,1024,256]{2,1,0:T(8,128)(2,1)}, u32[]{:S(2)}) copy-start(bf16[4,1024,256]{2,1,0:T(8,128)(2,1)} %all-gather.3.cloned.1.call-done.x) | copy-start | bytes 6291460
  143.7 34.6 %all-to-all-start.1 = ((bf16[64,16,256]{2,1,0:T(8,128)(2,1)}), bf16[64,16,256]{2,1,0:T(8,128)(2,1)S(1)}, u32[]{:S(2)}, u32[]{:S(2)}) async-start(bf16[64,16,256]{2,1,0:T(8,128)(2,1)} %bitcast.16), calls=%async_computation.2 | async-start | bytes 1048576 | tf_op jit(solution)/shard_map/all_to_all | solution.py:227
  178.3 31.8 %all-to-all-start.3 = ((bf16[64,16,256]{2,1,0:T(8,128)(2,1)}), bf16[64,16,256]{2,1,0:T(8,128)(2,1)S(1)}, u32[]{:S(2)}, u32[]{:S(2)}) async-start(bf16[64,16,256]{2,1,0:T(8,128)(2,1)} %bitcast.15), calls=%async_computation.5 | async-start | bytes 1048576 | tf_op jit(solution)/shard_map/all_to_all | solution.py:227
  188.9 1.2 copy-start.8
  190.1 1.2 copy-start.10
  191.3 1.2 copy-start.12
Sparse Core Ops, SparseCore 0:
  42.9 29.9 all-gather.2
  74.7 33.4 all-gather.4
  111.3 32.3 reduce-scatter.2
  146.3 31.9 reduce-scatter.4
